TPU v7x, 32 devices: a whole 2x2x4 slice. The times are simulated.
32 devices in a mesh: groups: 2 (over x), dev: 16 (over z, y, core).
Axes of the slice: x: 2, y: 2, z: 4, core: 2. Of those that a mesh axis runs over, the one named last changes fastest.
Arguments:
- request_query_rows: bfloat16 [96, 6144], P(('groups', 'dev')), parts along dimension 0, may hold values from -6 to 6
- new_kv: bfloat16 [96, 2048], P(('groups', 'dev')), parts along dimension 0, may hold values from -6 to 6
- kv_pool: bfloat16 [448, 16, 2048], P(('groups', 'dev')), parts along dimension 0, may hold values from -6 to 6
- page_table: int32 [32, 14], P(('groups', 'dev')), parts along dimension 0, may hold values from 0 to 13, each once within a row
- page_count: int32 [32, 3], P(('groups', 'dev')), parts along dimension 0, may hold values from 1 to 8, 14 in all within a row
- last_fill: int32 [32, 3], P(('groups', 'dev')), parts along dimension 0, may hold values from 1 to 16
- mig_slot: int32 [32, 3], P(('groups', 'dev')), parts along dimension 0, may hold values from 0 to 2, as said below
- residual: bfloat16 [96, 6144], P(('groups', 'dev')), parts along dimension 0, may hold values from -36 to 36
- norm_gain: float32 [6144], replicated, may hold values from 0.1 to 1.9
- route_ids: int32 [96, 2], P(('groups', 'dev')), parts along dimension 0, may hold values from 0 to 7, all different within a row; in each aligned block of 3 rows (0 to 2, 3 to 5, ...) at most 3 rows name the same one
- route_logit: bfloat16 [96, 2], P(('groups', 'dev')), parts along dimension 0, may hold values from -6 to 6
- w_gate: bfloat16 [6144, 2048], P(None, 'dev'), may hold values from -0.078125 to 0.078125
- w_up: bfloat16 [6144, 2048], P(None, 'dev'), may hold values from -0.078125 to 0.078125
- w_down: bfloat16 [2048, 6144], P('dev'), may hold values from -0.1875 to 0.1875
Outputs:
- layer_out: bfloat16 [96, 6144], P(('groups', 'dev')), parts along dimension 0
- arrived_cache: bfloat16 [96, 128, 2048], P(('groups', 'dev')), parts along dimension 0
There are 2 independent parts, one for each index of `groups`. A program takes and returns all parts, laid end to end along the dimension named above; an argument that names none is the same for every part. Nothing has to cross between parts.
Inputs may be any that keep to these rules, and one draw needn't show every extreme that they name: `mig_slot`: the entries of one instance's row differ. `route_ids`: each row names 2 different experts; among the 3 rows of one instance, before migration, no expert is named by more than 3 rows.
All inputs are finite; a program needn't handle non-finite values.
Results may differ from a plain program's by a relative error of at most 0.0028.
Values may be sent and summed in bfloat16 or wider, within the bound.
A program may use at most 64 MiB of HBM per device.

v0:
```python
import jax
import jax.numpy as jnp
from jax import lax
from jax.sharding import PartitionSpec as P

QUERY_HEADS = 48
KEY_VALUE_HEADS = 8
HEAD_SIZE = 128
MAXP = 8
NBITS = 3


epsilon = 1e-05


def swapped(block, axis, distance):
    count = lax.axis_size(axis)
    route = []
    for low in range(count):
        high = low | 1 << distance
        if high != low and high < count:
            route += [(low, high), (high, low)]
    return lax.ppermute(block, axis, route)


def own_cache(kv_pool, table_row, counts, last_fills):
    page_len = kv_pool.shape[1]
    pool_pages = table_row.shape[0]
    starts = jnp.cumsum(counts) - counts
    offsets = jnp.arange(MAXP, dtype=jnp.int32)
    page_slots = jnp.clip(starts[:, None] + offsets[None, :], 0, pool_pages - 1)
    physical = table_row[page_slots]
    blocks = kv_pool[physical]
    visible_positions = MAXP * page_len
    blocks = blocks.reshape(counts.shape[0], visible_positions, kv_pool.shape[2])
    length = (counts - 1) * page_len + last_fills
    inside = jnp.arange(visible_positions, dtype=jnp.int32)[None, :] < length[:, None]
    return (jnp.where(inside[:, :, None], blocks, jnp.zeros_like(blocks)), length)


def attend(request_query_rows, incoming_key_value, cache_row_block, length):
    total_row_count = request_query_rows.shape[0]
    visible_positions = cache_row_block.shape[1]
    query_group_count = QUERY_HEADS // KEY_VALUE_HEADS
    key_row_width = KEY_VALUE_HEADS * HEAD_SIZE
    query_by_group = request_query_rows.reshape(
        total_row_count, KEY_VALUE_HEADS, query_group_count, HEAD_SIZE
    )
    stored_key_rows = cache_row_block[:, :, :key_row_width].reshape(
        total_row_count, visible_positions, KEY_VALUE_HEADS, HEAD_SIZE
    )
    stored_value_rows = cache_row_block[:, :, key_row_width:].reshape(
        total_row_count, visible_positions, KEY_VALUE_HEADS, HEAD_SIZE
    )
    latest_key = incoming_key_value[:, :key_row_width].reshape(
        total_row_count, KEY_VALUE_HEADS, HEAD_SIZE
    )
    latest_value = incoming_key_value[:, key_row_width:].reshape(
        total_row_count, KEY_VALUE_HEADS, HEAD_SIZE
    )
    score_scale = HEAD_SIZE ** (-0.5)
    past_score = (
        jnp.einsum(
            "rgjd,rlgd->rgjl", query_by_group, stored_key_rows, preferred_element_type=jnp.float32
        )
        * score_scale
    )
    own_score = (
        jnp.einsum("rgjd,rgd->rgj", query_by_group, latest_key, preferred_element_type=jnp.float32)
        * score_scale
    )
    inside = jnp.arange(visible_positions, dtype=jnp.int32)[None, :] < length[:, None]
    past_score = jnp.where(inside[:, None, None, :], past_score, -jnp.inf)
    highest = jnp.maximum(jnp.max(past_score, axis=-1), own_score)
    past_exp = jnp.exp(past_score - highest[..., None])
    own_exp = jnp.exp(own_score - highest)
    denominator = jnp.sum(past_exp, axis=-1) + own_exp
    past_weight = (past_exp / denominator[..., None]).astype(jnp.bfloat16)
    own_weight = lax.optimization_barrier((own_exp / denominator).astype(jnp.bfloat16)).astype(
        jnp.float32
    )
    mixture = jnp.einsum(
        "rgjl,rlgd->rgjd", past_weight, stored_value_rows, preferred_element_type=jnp.float32
    )
    mixture = mixture + own_weight[..., None] * latest_value.astype(jnp.float32)[:, :, None, :]
    return mixture.reshape(total_row_count, QUERY_HEADS * HEAD_SIZE).astype(jnp.bfloat16)


def on_device(
    request_query_rows,
    new_kv,
    kv_pool,
    page_table,
    page_count,
    last_fill,
    mig_slot,
    residual,
    norm_gain,
    route_ids,
    route_logit,
    w_gate,
    w_up,
    w_down,
):
    cache_row_block, length = own_cache(kv_pool, page_table[0], page_count[0], last_fill[0])
    moved_slots = mig_slot[0]
    query_width = request_query_rows.shape[1]
    arrived = []
    for bit_index in range(NBITS):
        slot_index = moved_slots[bit_index]
        carried = jnp.concatenate([request_query_rows[slot_index], new_kv[slot_index]])
        received = swapped(
            (
                cache_row_block[slot_index],
                carried,
                residual[slot_index],
                route_logit[slot_index],
                route_ids[slot_index],
                length[slot_index][None],
            ),
            "dev",
            bit_index,
        )
        cache_row_block = cache_row_block.at[slot_index].set(received[0])
        request_query_rows = request_query_rows.at[slot_index].set(received[1][:query_width])
        new_kv = new_kv.at[slot_index].set(received[1][query_width:])
        residual = residual.at[slot_index].set(received[2])
        route_logit = route_logit.at[slot_index].set(received[3])
        route_ids = route_ids.at[slot_index].set(received[4])
        length = length.at[slot_index].set(received[5][0])
        arrived.append(received[0])
    attended = attend(request_query_rows, new_kv, cache_row_block, length)
    hidden_state = residual.astype(jnp.float32) + lax.optimization_barrier(attended).astype(
        jnp.float32
    )
    mean_square = jnp.mean(hidden_state * hidden_state, axis=1, keepdims=True)
    normed = (hidden_state * lax.rsqrt(mean_square + epsilon) * norm_gain).astype(jnp.bfloat16)
    route_probs = jax.nn.softmax(route_logit.astype(jnp.float32), axis=1)
    chosen_zero = route_ids == 0
    route_weight = jnp.sum(jnp.where(chosen_zero, route_probs, 0.0), axis=1)
    row_piece = lax.all_gather(normed, "dev", axis=0, tiled=True)
    gate_proj = jnp.dot(row_piece, w_gate, preferred_element_type=jnp.float32)
    up_proj = jnp.dot(row_piece, w_up, preferred_element_type=jnp.float32)
    acts = (jax.nn.silu(gate_proj) * up_proj).astype(jnp.bfloat16)
    summed = lax.psum_scatter(
        jnp.dot(acts, w_down, preferred_element_type=jnp.float32),
        "dev",
        scatter_dimension=0,
        tiled=True,
    )
    layer_out = (hidden_state + route_weight[:, None] * summed).astype(jnp.bfloat16)
    arrived_cache = jnp.stack(arrived)
    return (layer_out, arrived_cache)


def solution(mesh):
    placed = (
        P(("groups", "dev"), None),
        P(("groups", "dev"), None),
        P(("groups", "dev"), None, None),
        P(("groups", "dev"), None),
        P(("groups", "dev"), None),
        P(("groups", "dev"), None),
        P(("groups", "dev"), None),
        P(("groups", "dev"), None),
        P(),
        P(("groups", "dev"), None),
        P(("groups", "dev"), None),
        P(None, "dev"),
        P(None, "dev"),
        P("dev", None),
    )
    return jax.shard_map(
        on_device,
        mesh=mesh,
        in_specs=placed,
        out_specs=(P(("groups", "dev"), None), P(("groups", "dev"), None, None)),
        check_vma=False,
    )
```

profile of v0, /device:TPU:0, one launch (start us, length us, event | category | flops | bytes accessed | tf_op | source)
XLA Modules:
  0.0 221.0 jit_solution(773380101789942181)
XLA Ops:
  7.3 0.9 copy.75
  8.2 0.7 copy.76
  8.9 0.8 copy.77
  9.7 0.8 reduce-window.8
  10.5 0.7 bitcast_add_fusion
  11.5 0.7 gather_fusion
  12.4 0.7 fusion.37
  14.2 1.8 gather_fusion.1
  16.0 1.6 bitcast_select_fusion
  18.2 0.8 dynamic-slice_bitcast_fusion.2
  19.5 0.7 dynamic_slice.66
  20.4 0.5 collective-permute-start.6
  25.8 0.8 and_reduce_fusion
  26.6 0.8 and_reduce_fusion.3
  27.5 0.6 dynamic-slice.162
  28.8 1.4 fusion.24
  30.3 0.7 dynamic_slice.67
  30.9 3.0 %collective-permute-start.4 = (s32[1]{0:T(128)}, s32[1]{0:T(128)}, u32[]{:S(2)}, u32[]{:S(2)}) collective-permute-start(s32[1]{0:T(128)} %dynamic_slice.67), channel_id=1, source_target_pairs={{0,2},{2,0},{1,3},{3,1},{4,6},{6,4},{5,7},{7,5},{8,10},{10,8},{9,1... | collective-permute-start | bytes 20 | tf_op jit(solution)/shard_map/ppermute | solution.py:23
  33.9 0.6 broadcast_select_fusion.13
  34.5 0.9 collective-permute-done.4
  35.4 2.0 collective-permute-start.16
  37.5 1.4 fusion.25
  38.9 0.7 dynamic_slice.68
  39.5 1.6 collective-permute-start.5
  41.1 0.6 broadcast_select_fusion.11
  41.8 0.5 collective-permute-start.17
  42.3 0.6 broadcast_select_fusion.14
  43.1 1.5 collective-permute-start.13
  44.5 1.4 fusion.26
  46.0 0.6 broadcast_select_fusion.9
  47.1 0.6 broadcast_select_fusion.12
  47.8 1.6 collective-permute-start.14
  49.4 0.6 broadcast_select_fusion.5
  50.3 1.1 collective-permute-start.1
  51.4 0.6 broadcast_select_fusion.4
  52.3 0.6 broadcast_select_fusion.8
  53.1 1.1 collective-permute-start.7
  54.2 0.7 broadcast_select_fusion.3
  55.2 0.5 collective-permute-start.2
  55.7 1.2 collective-permute-done.7
  56.9 0.7 broadcast_select_fusion.2
  57.9 0.7 broadcast_select_fusion.7
  59.3 0.7 broadcast_select_fusion.1
  60.2 2.4 %collective-permute-done.8 = bf16[8192]{0:T(1024)(128)(2,1)S(1)} collective-permute-done((bf16[8192]{0:T(1024)(128)(2,1)S(1)}, bf16[8192]{0:T(1024)(128)(2,1)S(1)}, u32[]{:S(2)}, u32[]{:S(2)}) %collective-permute-start.8) | collective-permute-done | bytes 16416 | tf_op jit(solution)/shard_map/ppermute | solution.py:23
  62.6 1.9 select_dynamic-update-slice_fusion.2
  64.5 1.1 collective-permute-start.10
  65.6 0.7 broadcast_select_fusion
  66.3 7.5 %collective-permute-done.10 = bf16[128,2048]{1,0:T(8,128)(2,1)S(1)} collective-permute-done((bf16[128,2048]{1,0:T(8,128)(2,1)S(1)}, bf16[128,2048]{1,0:T(8,128)(2,1)S(1)}, u32[]{:S(2)}, u32[]{:S(2)}) %collective-permute-start.10) | collective-permute-done | bytes 524320 | tf_op jit(solution)/shard_map/ppermute | solution.py:23
  73.8 0.9 select_dynamic-update-slice_fusion.1
  74.6 0.8 dynamic-slice_bitcast_fusion
  75.9 0.6 broadcast_select_fusion.6
  77.2 7.8 %collective-permute-done.11 = bf16[128,2048]{1,0:T(8,128)(2,1)} collective-permute-done((bf16[128,2048]{1,0:T(8,128)(2,1)}, bf16[128,2048]{1,0:T(8,128)(2,1)}, u32[]{:S(2)}, u32[]{:S(2)}) %collective-permute-start.11) | collective-permute-done | bytes 524320 | tf_op jit(solution)/shard_map/ppermute | solution.py:23
  85.0 1.9 select_dynamic-update-slice_fusion
  86.9 1.3 fusion.35
  88.2 2.4 %copy.37 = bf16[3,128,1024]{1,2,0:T(8,128)(2,1)} copy(bf16[3,128,1024]{2,1,0:T(8,128)(2,1)} %get-tuple-element.262) | data formatting | bytes 1572864 | tf_op jit(solution)/shard_map/slice | solution.py:52
  91.6 1.7 fusion
  93.6 22.2 %all-gather = bf16[16,3,6144]{2,1,0:T(4,128)(2,1)S(1)} all-gather(bf16[1,3,6144]{2,1,0:T(4,128)(2,1)S(1)} %fusion.6), channel_id=1, replica_groups=mesh['groups'=2,'dev'=16] {'dev'}, dimensions={0}, use_global_device_ids=true | all-gather | bytes 626688 | tf_op jit(solution)/shard_map/all_gather | solution.py:141
  115.8 0.5 reshape.776
  116.3 1.8 fusion.39
  118.1 3.2 %fusion.2 = f32[48,6144]{1,0:T(8,128)} fusion(bf16[128,6144]{1,0:T(8,128)(2,1)S(1)} %copy-done, bf16[48,6144]{1,0:T(8,128)(2,1)S(1)} %reshape.776, bf16[6144,128]{1,0:T(8,128)(2,1)} %param.68, f32[48,128]{1,0:T(8,128)S(1)} %fusion.39), kind=kOutput, calls=%fused_computation.9 | convolution fusion | flops 151031808 | bytes 4939776 | tf_op jit(solution)/shard_map/dot_general | solution.py:146
  121.4 0.6 broadcast_select_fusion.10
  122.3 2.5 %pad_maximum_fusion = bf16[3,128,2048]{2,1,0:T(8,128)(2,1)} fusion(bf16[1,128,2048]{2,1,0:T(8,128)(2,1)} %bitcast.17, bf16[1,128,2048]{2,1,0:T(8,128)(2,1)S(1)} %bitcast.87, bf16[1,128,2048]{2,1,0:T(8,128)(2,1)} %bitcast.13), kind=kLoop, calls=%fused_computation.2 | loop fusion | flops 1572864 | bytes 3145728 | tf_op jit(solution)/shard_map/stack | solution.py:152
  124.8 87.7 %all-reduce.3.cloned.1.call-done = f32[48,6144]{1,0:T(8,128)} async-done(((f32[48,6144]{1,0:T(8,128)}), f32[48,6144]{1,0:T(8,128)}) %all-reduce.3.cloned.1.call-update) | async-done | bytes 1179664
  212.5 1.7 fusion.4
  (118 shorter events, 7.9 us)
Async XLA Ops:
  7.2 110.9 %copy-start = (bf16[128,6144]{1,0:T(8,128)(2,1)S(1)}, bf16[128,6144]{1,0:T(8,128)(2,1)}, u32[]{:S(2)}) copy-start(bf16[128,6144]{1,0:T(8,128)(2,1)} %param.69) | copy-start | bytes 4718596
  7.2 4.3 %copy-start.1 = (s32[1,14]{1,0:T(1,128)S(1)}, s32[1,14]{1,0:T(1,128)}, u32[]{:S(2)}) copy-start(s32[1,14]{1,0:T(1,128)} %param.59) | copy-start | bytes 172
  7.2 7.0 %copy-start.3 = (bf16[14,16,2048]{2,1,0:T(8,128)(2,1)S(1)}, bf16[14,16,2048]{2,1,0:T(8,128)(2,1)}, u32[]{:S(2)}) copy-start(bf16[14,16,2048]{2,1,0:T(8,128)(2,1)} %param.58) | copy-start | bytes 2752516
  7.2 5.2 %copy-start.7 = (s32[1,3]{1,0:T(1,128)S(1)}, s32[1,3]{1,0:T(1,128)}, u32[]{:S(2)}) copy-start(s32[1,3]{1,0:T(1,128)} %param.62) | copy-start | bytes 40
  7.2 205.3 %all-reduce.3.cloned.1.call-start = ((), (), s32[]{:S(2)}) async-start(), calls=%async_computation | async-start | bytes 2359296
  16.0 5.1 %copy-start.11 = (bf16[3,2]{0,1:T(2,128)(2,1)S(1)}, bf16[3,2]{0,1:T(2,128)(2,1)}, u32[]{:S(2)}) copy-start(bf16[3,2]{0,1:T(2,128)(2,1)} %param.66) | copy-start | bytes 40
  16.0 9.8 %copy-start.10 = (s32[3]{0:T(128)S(1)}, s32[3]{0:T(128)}, u32[]{:S(2)}) copy-start(s32[3]{0:T(128)} %constant.454.clone.1) | copy-start | bytes 40
  16.0 10.6 %copy-start.9 = (s32[2]{0:T(128)S(1)}, s32[2]{0:T(128)}, u32[]{:S(2)}) copy-start(s32[2]{0:T(128)} %constant.446.clone.1) | copy-start | bytes 28
  16.0 11.4 %copy-start.8 = (s32[3,2]{0,1:T(2,128)S(1)}, s32[3,2]{0,1:T(2,128)}, u32[]{:S(2)}) copy-start(s32[3,2]{0,1:T(2,128)} %param.65) | copy-start | bytes 76
  16.0 11.5 %copy-start.12 = (u32[32]{0:T(128)S(1)}, u32[32]{0:T(128)}, u32[]{:S(2)}) copy-start(u32[32]{0:T(128)} %constant.474) | copy-start | bytes 388
  19.1 43.5 %collective-permute-start.9 = (bf16[128,2048]{1,0:T(8,128)(2,1)}, bf16[128,2048]{1,0:T(8,128)(2,1)}, u32[]{:S(2)}, u32[]{:S(2)}) collective-permute-start(bf16[128,2048]{1,0:T(8,128)(2,1)} %dynamic-slice_bitcast_fusion.2), channel_id=1, source_target_pairs={{0,1},{1,0},{2,3},{3,2},{4,5},{5,4},{6,7},{7,6},{8,9},{9,8},{10,11... | collective-permute-start | bytes 1572872 | tf_op jit(solution)/shard_map/ppermute | solution.py:23
  20.2 8.5 %collective-permute-start.3 = (s32[1]{0:T(128)}, s32[1]{0:T(128)}, u32[]{:S(2)}, u32[]{:S(2)}) collective-permute-start(s32[1]{0:T(128)} %dynamic_slice.66), channel_id=1, source_target_pairs={{0,1},{1,0},{2,3},{3,2},{4,5},{5,4},{6,7},{7,6},{8,9},{9,8},{10,11... | collective-permute-start | bytes 20 | tf_op jit(solution)/shard_map/ppermute | solution.py:23
  20.4 31.0 %collective-permute-start.6 = (bf16[8192]{0:T(1024)(128)(2,1)S(1)}, bf16[8192]{0:T(1024)(128)(2,1)S(1)}, u32[]{:S(2)}, u32[]{:S(2)}) collective-permute-start(bf16[8192]{0:T(1024)(128)(2,1)S(1)} %pad_maximum_fusion.1), channel_id=1, source_target_pairs={{0,1},{1,0},{2,3},{3,2},{4,5},{5,4},{6,7},{7,6},{8,9},{9,8},{10,11... | collective-permute-start | bytes 49160 | tf_op jit(solution)/shard_map/ppermute | solution.py:23
  21.0 28.4 %collective-permute-start = (bf16[6144]{0:T(1024)(128)(2,1)S(1)}, bf16[6144]{0:T(1024)(128)(2,1)S(1)}, u32[]{:S(2)}, u32[]{:S(2)}) collective-permute-start(bf16[6144]{0:T(1024)(128)(2,1)S(1)} %dynamic-slice_reduce_fusion.5), channel_id=1, source_target_pairs={{0,1},{1,0},{2,3},{3,2},{4,5},{5,4},{6,7},{7,6},{8,9},{9,8},{10,11... | collective-permute-start | bytes 36872 | tf_op jit(solution)/shard_map/ppermute | solution.py:23
  21.2 9.7 %collective-permute-start.15 = (bf16[2]{0:T(256)(128)(2,1)S(1)}, bf16[2]{0:T(256)(128)(2,1)S(1)}, u32[]{:S(2)}, u32[]{:S(2)}) collective-permute-start(bf16[2]{0:T(256)(128)(2,1)S(1)} %fusion.30), channel_id=1, source_target_pairs={{0,1},{1,0},{2,3},{3,2},{4,5},{5,4},{6,7},{7,6},{8,9},{9,8},{10,11... | collective-permute-start | bytes 20 | tf_op jit(solution)/shard_map/ppermute | solution.py:23
  28.7 13.1 %collective-permute-start.12 = (s32[2]{0:T(128)S(1)}, s32[2]{0:T(128)S(1)}, u32[]{:S(2)}, u32[]{:S(2)}) collective-permute-start(s32[2]{0:T(128)S(1)} %fusion.27), channel_id=1, source_target_pairs={{0,1},{1,0},{2,3},{3,2},{4,5},{5,4},{6,7},{7,6},{8,9},{9,8},{10,11... | collective-permute-start | bytes 32 | tf_op jit(solution)/shard_map/ppermute | solution.py:23
  30.9 4.5 %collective-permute-start.4 = (s32[1]{0:T(128)}, s32[1]{0:T(128)}, u32[]{:S(2)}, u32[]{:S(2)}) collective-permute-start(s32[1]{0:T(128)} %dynamic_slice.67), channel_id=1, source_target_pairs={{0,2},{2,0},{1,3},{3,1},{4,6},{6,4},{5,7},{7,5},{8,10},{10,8},{9,1... | collective-permute-start | bytes 20 | tf_op jit(solution)/shard_map/ppermute | solution.py:23
  35.4 4.1 %collective-permute-start.16 = (bf16[2]{0:T(256)(128)(2,1)S(1)}, bf16[2]{0:T(256)(128)(2,1)S(1)}, u32[]{:S(2)}, u32[]{:S(2)}) collective-permute-start(bf16[2]{0:T(256)(128)(2,1)S(1)} %fusion.31), channel_id=1, source_target_pairs={{0,2},{2,0},{1,3},{3,1},{4,6},{6,4},{5,7},{7,5},{8,10},{10,8},{9,1... | collective-permute-start | bytes 20 | tf_op jit(solution)/shard_map/ppermute | solution.py:23
  39.5 3.6 %collective-permute-start.5 = (s32[1]{0:T(128)}, s32[1]{0:T(128)}, u32[]{:S(2)}, u32[]{:S(2)}) collective-permute-start(s32[1]{0:T(128)} %dynamic_slice.68), channel_id=1, source_target_pairs={{0,4},{4,0},{1,5},{5,1},{2,6},{6,2},{3,7},{7,3},{8,12},{12,8},{9,1... | collective-permute-start | bytes 20 | tf_op jit(solution)/shard_map/ppermute | solution.py:23
  41.8 4.2 %collective-permute-start.17 = (bf16[2]{0:T(256)(128)(2,1)S(1)}, bf16[2]{0:T(256)(128)(2,1)S(1)}, u32[]{:S(2)}, u32[]{:S(2)}) collective-permute-start(bf16[2]{0:T(256)(128)(2,1)S(1)} %fusion.32), channel_id=1, source_target_pairs={{0,4},{4,0},{1,5},{5,1},{2,6},{6,2},{3,7},{7,3},{8,12},{12,8},{9,1... | collective-permute-start | bytes 20 | tf_op jit(solution)/shard_map/ppermute | solution.py:23
  43.1 4.0 %collective-permute-start.13 = (s32[2]{0:T(128)S(1)}, s32[2]{0:T(128)S(1)}, u32[]{:S(2)}, u32[]{:S(2)}) collective-permute-start(s32[2]{0:T(128)S(1)} %fusion.28), channel_id=1, source_target_pairs={{0,2},{2,0},{1,3},{3,1},{4,6},{6,4},{5,7},{7,5},{8,10},{10,8},{9,1... | collective-permute-start | bytes 32 | tf_op jit(solution)/shard_map/ppermute | solution.py:23
  47.8 73.6 %collective-permute-start.14 = (s32[2]{0:T(128)S(1)}, s32[2]{0:T(128)S(1)}, u32[]{:S(2)}, u32[]{:S(2)}) collective-permute-start(s32[2]{0:T(128)S(1)} %fusion.29), channel_id=1, source_target_pairs={{0,4},{4,0},{1,5},{5,1},{2,6},{6,2},{3,7},{7,3},{8,12},{12,8},{9,1... | collective-permute-start | bytes 32 | tf_op jit(solution)/shard_map/ppermute | solution.py:23
  50.3 3.8 %collective-permute-start.1 = (bf16[6144]{0:T(1024)(128)(2,1)S(1)}, bf16[6144]{0:T(1024)(128)(2,1)S(1)}, u32[]{:S(2)}, u32[]{:S(2)}) collective-permute-start(bf16[6144]{0:T(1024)(128)(2,1)S(1)} %dynamic-slice_reduce_fusion.4), channel_id=1, source_target_pairs={{0,2},{2,0},{1,3},{3,1},{4,6},{6,4},{5,7},{7,5},{8,10},{10,8},{9,1... | collective-permute-start | bytes 36872 | tf_op jit(solution)/shard_map/ppermute | solution.py:23
  53.1 3.8 %collective-permute-start.7 = (bf16[8192]{0:T(1024)(128)(2,1)S(1)}, bf16[8192]{0:T(1024)(128)(2,1)S(1)}, u32[]{:S(2)}, u32[]{:S(2)}) collective-permute-start(bf16[8192]{0:T(1024)(128)(2,1)S(1)} %pad_maximum_fusion.2), channel_id=1, source_target_pairs={{0,2},{2,0},{1,3},{3,1},{4,6},{6,4},{5,7},{7,5},{8,10},{10,8},{9,1... | collective-permute-start | bytes 49160 | tf_op jit(solution)/shard_map/ppermute | solution.py:23
  55.2 4.1 %collective-permute-start.2 = (bf16[6144]{0:T(1024)(128)(2,1)S(1)}, bf16[6144]{0:T(1024)(128)(2,1)S(1)}, u32[]{:S(2)}, u32[]{:S(2)}) collective-permute-start(bf16[6144]{0:T(1024)(128)(2,1)S(1)} %dynamic-slice_reduce_fusion.3), channel_id=1, source_target_pairs={{0,4},{4,0},{1,5},{5,1},{2,6},{6,2},{3,7},{7,3},{8,12},{12,8},{9,1... | collective-permute-start | bytes 36872 | tf_op jit(solution)/shard_map/ppermute | solution.py:23
  58.8 3.8 %collective-permute-start.8 = (bf16[8192]{0:T(1024)(128)(2,1)S(1)}, bf16[8192]{0:T(1024)(128)(2,1)S(1)}, u32[]{:S(2)}, u32[]{:S(2)}) collective-permute-start(bf16[8192]{0:T(1024)(128)(2,1)S(1)} %pad_maximum_fusion.3), channel_id=1, source_target_pairs={{0,4},{4,0},{1,5},{5,1},{2,6},{6,2},{3,7},{7,3},{8,12},{12,8},{9,1... | collective-permute-start | bytes 49160 | tf_op jit(solution)/shard_map/ppermute | solution.py:23
  64.5 9.2 %collective-permute-start.10 = (bf16[128,2048]{1,0:T(8,128)(2,1)S(1)}, bf16[128,2048]{1,0:T(8,128)(2,1)S(1)}, u32[]{:S(2)}, u32[]{:S(2)}) collective-permute-start(bf16[128,2048]{1,0:T(8,128)(2,1)S(1)} %dynamic-slice_bitcast_fusion.1), channel_id=1, source_target_pairs={{0,2},{2,0},{1,3},{3,1},{4,6},{6,4},{5,7},{7,5},{8,10},{10,8},{9,1... | collective-permute-start | bytes 1572872 | tf_op jit(solution)/shard_map/ppermute | solution.py:23
  73.8 0.9 copy-start.4
  75.5 9.5 %collective-permute-start.11 = (bf16[128,2048]{1,0:T(8,128)(2,1)}, bf16[128,2048]{1,0:T(8,128)(2,1)}, u32[]{:S(2)}, u32[]{:S(2)}) collective-permute-start(bf16[128,2048]{1,0:T(8,128)(2,1)} %dynamic-slice_bitcast_fusion), channel_id=1, source_target_pairs={{0,4},{4,0},{1,5},{5,1},{2,6},{6,2},{3,7},{7,3},{8,12},{12,8},{9,1... | collective-permute-start | bytes 1572872 | tf_op jit(solution)/shard_map/ppermute | solution.py:23
  88.2 2.4 %copy-start.2 = (bf16[3,128,1024]{2,1,0:T(8,128)(2,1)S(1)}, bf16[3,128,1024]{2,1,0:T(8,128)(2,1)}, u32[]{:S(2)}) copy-start(bf16[3,128,1024]{2,1,0:T(8,128)(2,1)} %get-tuple-element.261) | copy-start | bytes 2359300
  91.0 2.6 %copy-start.6 = (f32[6144]{0:T(1024)S(1)}, f32[6144]{0:T(1024)}, u32[]{:S(2)}) copy-start(f32[6144]{0:T(1024)} %param.64) | copy-start | bytes 73732
  118.1 4.1 %copy-start.5 = (bf16[128,2048]{1,0:T(8,128)(2,1)S(1)}, bf16[128,2048]{1,0:T(8,128)(2,1)}, u32[]{:S(2)}) copy-start(bf16[128,2048]{1,0:T(8,128)(2,1)} %copy-done.4) | copy-start | bytes 1572868
Sparse Core Ops, SparseCore 0:
  121.5 90.9 all-reduce.2
where the time goes:
time: 222 us; the launch traced here: 221 us
  waiting for transfers between devices  108 us (49%)
  other arithmetic  28.6 us (13%)
  blocking collectives  22.2 us (10%)
  between operations  20.9 us (9%)
  local copies, waits for them, and re-layouts  17.8 us (8%)
  starting transfers between devices  16.7 us (8%)
  matrix products  7.23 us (3%)
    unnamed x2, waiting for transfers between devices  87.7 us
    all_gather x1, blocking collectives, on_device(): row_piece = lax.all_gather(normed, 'dev', axis=0, tiled=True)  22.2 us
    ppermute x18, waiting for transfers between devices, swapped(): return lax.ppermute(block, axis, route)  19.9 us
    ppermute x18, starting transfers between devices, swapped(): return lax.ppermute(block, axis, route)  16.7 us
    another operation x18, other arithmetic  11.9 us
    scatter x3, other arithmetic, on_device(): cache_row_block = cache_row_block.at[slot_index].set(received[0])  4.65 us
  transfers between devices with their start and end apart: 19, of which 7 were waited for; matrix products, arithmetic and copies ran while one was open for 19% of the time, Pallas kernels for 0%

commit v1 on v0

v1 whole, which is shorter than its diff:
```python
import functools

import jax
import jax.numpy as jnp
from jax import lax
from jax.experimental import pallas as pl
from jax.experimental.pallas import tpu as pltpu
from jax.sharding import PartitionSpec as P

KEY_VALUE_HEADS = 8
LANES = 128
NBITS = 3
REQ = 3

epsilon = 1e-05


def flipped(value, bit):
    return value + bit - 2 * bit * ((value // bit) % 2)


def layer_kernel(
    n,
    bits,
    maxp,
    q_ref,
    nkv_ref,
    pool_hbm,
    table,
    counts,
    fills,
    mig,
    res_ref,
    gain_ref,
    ids_ref,
    logit_ref,
    wg_hbm,
    wu_hbm,
    wd_hbm,
    out_ref,
    arr_ref,
    pool,
    cache,
    wg,
    wu,
    wd,
    qs,
    kvs,
    rs,
    route,
    hid_send,
    hid_recv,
    gathered,
    wide,
    rows_x,
    shares,
    rs_send,
    rs_recv,
    fin,
    local_sem,
    cache_send_sem,
    cache_recv_sem,
    hid_send_sem,
    hid_recv_sem,
    ag_send_sem,
    ag_recv_sem,
    rs_send_sem,
    rs_recv_sem,
):
    me = lax.axis_index("dev")
    page = pool.shape[1]
    width = pool.shape[2]
    pool_pages = pool.shape[0]
    chunks = q_ref.shape[1] // LANES
    kvc = nkv_ref.shape[1] // LANES
    group = chunks // KEY_VALUE_HEADS
    key_width = KEY_VALUE_HEADS * LANES
    block = REQ * chunks
    scale = LANES ** (-0.5)

    pool_copy = pltpu.make_async_copy(pool_hbm, pool, local_sem.at[0])
    pool_copy.start()
    weight_copies = [
        pltpu.make_async_copy(src, dst, local_sem.at[1 + i])
        for i, (src, dst) in enumerate(((wg_hbm, wg), (wu_hbm, wu), (wd_hbm, wd)))
    ]
    for copy in weight_copies:
        copy.start()

    barrier = pltpu.get_barrier_semaphore()
    partners = [flipped(me, 1 << k) for k in range(bits)]
    for partner in partners:
        pl.semaphore_signal(
            barrier, inc=1, device_id={"dev": partner}, device_id_type=pl.DeviceIdType.MESH
        )

    pos = 0
    for k in range(bits):
        pos = pos + ((me // (1 << k)) % 2) * (1 << (bits - 1 - k))

    qf = q_ref[...].astype(jnp.float32)
    rf = res_ref[...].astype(jnp.float32)
    for c in range(chunks):
        qs[pl.ds(c, REQ, stride=chunks), :] = qf[:, c * LANES : (c + 1) * LANES]
        rs[pl.ds(c, REQ, stride=chunks), :] = rf[:, c * LANES : (c + 1) * LANES]
    kf = nkv_ref[...].astype(jnp.float32)
    for c in range(kvc):
        kvs[pl.ds(c, REQ, stride=kvc), :] = kf[:, c * LANES : (c + 1) * LANES]
    logits = logit_ref[...].astype(jnp.float32)
    e = jnp.exp(logits - jnp.max(logits, axis=1, keepdims=True))
    probs = e / jnp.sum(e, axis=1, keepdims=True)
    chosen = jnp.sum(jnp.where(ids_ref[...] == 0, probs, 0.0), axis=1, keepdims=True)
    route[...] = jnp.zeros_like(route)
    route[pl.ds(0, REQ), :] = jnp.broadcast_to(chosen, (REQ, LANES))

    def picked(slot, values):
        chosen_value = values[REQ - 1]
        for i in range(REQ - 2, -1, -1):
            chosen_value = jnp.where(slot == i, values[i], chosen_value)
        return chosen_value

    spans = [(counts[0, s] - 1) * page + fills[0, s] for s in range(REQ)]
    firsts = [jnp.int32(0)]
    for s in range(REQ - 1):
        firsts.append(firsts[-1] + counts[0, s])
    slots = [mig[0, b] for b in range(NBITS)]
    lengths = [picked(slot, spans) for slot in slots]
    starts = [picked(slot, firsts) for slot in slots]
    visible = maxp * page
    pool_rows = pool_pages * page
    row = lax.broadcasted_iota(jnp.int32, (visible, LANES), 0)
    row_page = row // page
    lane = lax.broadcasted_iota(jnp.int32, (visible, pool_rows), 1)

    def chooser(b):
        ordinal = row_page + starts[b]
        target = jnp.zeros((visible, LANES), jnp.int32)
        for j in range(pool_pages):
            target = jnp.where(ordinal == j, table[0, j], target)
        target = target * page + (row - row_page * page)
        target = jnp.where(row < lengths[b], target, -1)[:, :1]
        return jnp.where(lane == target, 1.0, 0.0).astype(jnp.bfloat16)

    choosers = [chooser(b) for b in range(NBITS)]

    pool_copy.wait()
    pl.semaphore_wait(barrier, bits)

    cache_copies = {}
    for b in (1, 2, 0):
        cache[b] = jnp.dot(
            choosers[b], pool[...].reshape(pool_rows, width), preferred_element_type=jnp.float32
        ).astype(jnp.bfloat16)
        cache_copies[b] = pltpu.make_async_remote_copy(
            src_ref=cache.at[b],
            dst_ref=arr_ref.at[b],
            send_sem=cache_send_sem.at[b],
            recv_sem=cache_recv_sem.at[b],
            device_id={"dev": partners[b]},
            device_id_type=pl.DeviceIdType.MESH,
        )
        cache_copies[b].start()

    head = lax.broadcasted_iota(jnp.int32, (chunks, LANES), 0)
    position = lax.broadcasted_iota(jnp.int32, (chunks, maxp * page), 1)

    def spread(parts):
        total = parts(0)
        for g in range(1, KEY_VALUE_HEADS):
            total = jnp.where(head >= g * group, parts(g), total)
        return total

    hid_copies = []
    for b in range(NBITS):
        slot = slots[b]
        qrow = picked(slot, [qs[s * chunks : (s + 1) * chunks, :] for s in range(REQ)])
        q16 = qrow.astype(jnp.bfloat16)
        nk, nv = [
            picked(slot, [kvs[pl.ds(s * kvc + at, KEY_VALUE_HEADS), :] for s in range(REQ)])
            for at in (0, KEY_VALUE_HEADS)
        ]
        score = spread(
            lambda g: lax.dot_general(
                q16,
                cache[b, :, g * LANES : (g + 1) * LANES],
                (((1,), (1,)), ((), ())),
                preferred_element_type=jnp.float32,
            )
        )
        new_key = spread(lambda g: jnp.broadcast_to(nk[g : g + 1, :], (chunks, LANES)))
        new_value = spread(lambda g: jnp.broadcast_to(nv[g : g + 1, :], (chunks, LANES)))
        own_score = jnp.sum(qrow * new_key, axis=1, keepdims=True) * scale
        score = jnp.where(position < lengths[b], score * scale, -jnp.inf)
        highest = jnp.maximum(jnp.max(score, axis=1, keepdims=True), own_score)
        past = jnp.exp(score - highest)
        mine = jnp.exp(own_score - highest)
        denominator = jnp.sum(past, axis=1, keepdims=True) + mine
        weight = (past / denominator).astype(jnp.bfloat16)
        own_weight = (mine / denominator).astype(jnp.bfloat16).astype(jnp.float32)
        mixture = spread(
            lambda g: jnp.dot(
                weight,
                cache[b, :, key_width + g * LANES : key_width + (g + 1) * LANES],
                preferred_element_type=jnp.float32,
            )
        )
        attended = (mixture + own_weight * new_value).astype(jnp.bfloat16)
        rest = picked(slot, [rs[s * chunks : (s + 1) * chunks, :] for s in range(REQ)])
        hidden = rest + attended.astype(jnp.float32)
        mean_square = jnp.sum(
            jnp.sum(hidden * hidden, axis=1, keepdims=True), axis=0, keepdims=True
        ) * (1.0 / (chunks * LANES))
        normed = hidden * lax.rsqrt(mean_square + epsilon) * gain_ref[...]
        gathered[pl.ds(pl.multiple_of(pos * block + b * chunks, 16), chunks), :] = normed.astype(
            jnp.bfloat16
        )
        hid_send[b, pl.ds(0, chunks), :] = hidden
        hid_send[b, pl.ds(chunks, 8), :] = jnp.broadcast_to(
            picked(slot, [route[s : s + 1, :] for s in range(REQ)]), (8, LANES)
        )
        copy = pltpu.make_async_remote_copy(
            src_ref=hid_send.at[b],
            dst_ref=hid_recv.at[b],
            send_sem=hid_send_sem.at[b],
            recv_sem=hid_recv_sem.at[b],
            device_id={"dev": partners[b]},
            device_id_type=pl.DeviceIdType.MESH,
        )
        hid_copies.append(copy)

    def widen(first, amount):
        def one(i, carry):
            source = first + i
            for b in range(NBITS):
                target = flipped(source, 1 << (bits - 1 - b))
                wide[pl.ds(pl.multiple_of((target * REQ + b) * chunks, 16), chunks), :] = gathered[
                    pl.ds(pl.multiple_of((source * REQ + b) * chunks, 16), chunks), :
                ].astype(jnp.float32)
            return carry

        lax.fori_loop(0, amount, one, 0)

    ag_copies = []
    for step in range(bits):
        k = bits - 1 - step
        size = 1 << step
        have = (pos // size) * size
        rows = pl.ds(pl.multiple_of(have * block, 16), size * block)
        copy = pltpu.make_async_remote_copy(
            src_ref=gathered.at[rows, :],
            dst_ref=gathered.at[rows, :],
            send_sem=ag_send_sem.at[step],
            recv_sem=ag_recv_sem.at[step],
            device_id={"dev": partners[k]},
            device_id_type=pl.DeviceIdType.MESH,
        )
        copy.start()
        ag_copies.append(copy)
        if step == 0:
            for hid in hid_copies:
                hid.start()
            widen(pos, 1)
        else:
            widen(other, size // 2)
        copy.wait_recv()
        other = flipped(have // size, 1) * size
    widen(other, n // 2)

    count = n * REQ
    for c in range(chunks):
        rows_x[:, c * LANES : (c + 1) * LANES] = wide[pl.ds(c, count, stride=chunks), :].astype(
            jnp.bfloat16
        )
    weight_copies[0].wait()
    weight_copies[1].wait()
    x = rows_x[...]
    gate = jnp.dot(x, wg[...], preferred_element_type=jnp.float32)
    up = jnp.dot(x, wu[...], preferred_element_type=jnp.float32)
    acts = (gate * (1.0 / (1.0 + jnp.exp(-gate))) * up).astype(jnp.bfloat16)
    weight_copies[2].wait()
    piece = 4
    for c in range(0, chunks, piece):
        y = jnp.dot(
            acts, wd[:, c * LANES : (c + piece) * LANES], preferred_element_type=jnp.float32
        )
        for j in range(piece):
            shares[pl.ds(c + j, count, stride=chunks), :] = y[:, j * LANES : (j + 1) * LANES]

    rs_copies = []
    offset = 0
    for k in range(bits):
        half = n >> (k + 1)
        mine_at = (pos // half) * half
        theirs_at = flipped(pos // half, 1) * half
        slab = pl.ds(offset * block, half * block)
        rs_send[slab, :] = shares[
            pl.ds(pl.multiple_of(theirs_at * block, 16), half * block), :
        ].astype(jnp.bfloat16)
        copy = pltpu.make_async_remote_copy(
            src_ref=rs_send.at[slab, :],
            dst_ref=rs_recv.at[slab, :],
            send_sem=rs_send_sem.at[k],
            recv_sem=rs_recv_sem.at[k],
            device_id={"dev": partners[k]},
            device_id_type=pl.DeviceIdType.MESH,
        )
        copy.start()
        rs_copies.append(copy)
        copy.wait_recv()
        keep = pl.ds(pl.multiple_of(mine_at * block, 16), half * block)
        shares[keep, :] = shares[keep, :] + rs_recv[slab, :].astype(jnp.float32)
        offset += half

    done = []
    for b in range(NBITS):
        hid_copies[b].wait_recv()
        summed = shares[pl.ds(pl.multiple_of(pos * block + b * chunks, 16), chunks), :]
        done.append(hid_recv[b, pl.ds(0, chunks), :] + hid_recv[b, pl.ds(chunks, 1), :] * summed)
    for s in range(REQ):
        row = jnp.where(slots[0] == s, done[0], jnp.where(slots[1] == s, done[1], done[2]))
        fin[pl.ds(s * chunks, chunks), :] = row
    for c in range(chunks):
        out_ref[:, c * LANES : (c + 1) * LANES] = fin[pl.ds(c, REQ, stride=chunks), :].astype(
            jnp.bfloat16
        )

    for copy in ag_copies + rs_copies + hid_copies:
        copy.wait_send()
    for b in range(NBITS):
        cache_copies[b].wait()


def on_device(
    request_query_rows,
    new_kv,
    kv_pool,
    page_table,
    page_count,
    last_fill,
    mig_slot,
    residual,
    norm_gain,
    route_ids,
    route_logit,
    w_gate,
    w_up,
    w_down,
):
    n = lax.axis_size("dev")
    bits = n.bit_length() - 1
    maxp = 8
    page, width = kv_pool.shape[1:]
    d = residual.shape[1]
    chunks = d // LANES
    kvc = width // LANES
    rows = n * REQ * chunks
    block = REQ * chunks
    hidden_units = w_down.shape[0]
    vmem = pl.BlockSpec(memory_space=pltpu.VMEM)
    smem = pl.BlockSpec(memory_space=pltpu.SMEM)
    anywhere = pl.BlockSpec(memory_space=pl.ANY)
    f32, bf16 = jnp.float32, jnp.bfloat16
    dma = pltpu.SemaphoreType.DMA
    layer_out, arrived = pl.pallas_call(
        functools.partial(layer_kernel, n, bits, maxp),
        out_shape=(
            jax.ShapeDtypeStruct((REQ, d), bf16),
            jax.ShapeDtypeStruct((NBITS, maxp * page, width), bf16),
        ),
        in_specs=[
            vmem, vmem, anywhere, smem, smem, smem, smem, vmem, vmem, vmem, vmem,
            anywhere, anywhere, anywhere,
        ],
        out_specs=(vmem, anywhere),
        scratch_shapes=[
            pltpu.VMEM(kv_pool.shape, bf16),
            pltpu.VMEM((NBITS, maxp * page, width), bf16),
            pltpu.VMEM(w_gate.shape, bf16),
            pltpu.VMEM(w_up.shape, bf16),
            pltpu.VMEM(w_down.shape, bf16),
            pltpu.VMEM((block, LANES), f32),
            pltpu.VMEM((REQ * kvc, LANES), f32),
            pltpu.VMEM((block, LANES), f32),
            pltpu.VMEM((8, LANES), f32),
            pltpu.VMEM((NBITS, chunks + 8, LANES), f32),
            pltpu.VMEM((NBITS, chunks + 8, LANES), f32),
            pltpu.VMEM((rows, LANES), bf16),
            pltpu.VMEM((rows, LANES), f32),
            pltpu.VMEM((n * REQ, d), bf16),
            pltpu.VMEM((rows, LANES), f32),
            pltpu.VMEM(((n - 1) * block, LANES), bf16),
            pltpu.VMEM(((n - 1) * block, LANES), bf16),
            pltpu.VMEM((block, LANES), f32),
            dma((4,)),
            dma((NBITS,)),
            dma((NBITS,)),
            dma((NBITS,)),
            dma((NBITS,)),
            dma((bits,)),
            dma((bits,)),
            dma((bits,)),
            dma((bits,)),
        ],
        compiler_params=pltpu.CompilerParams(
            collective_id=0, has_side_effects=True, vmem_limit_bytes=56 * 1024 * 1024
        ),
    )(
        request_query_rows,
        new_kv,
        kv_pool,
        page_table,
        page_count,
        last_fill,
        mig_slot,
        residual,
        norm_gain.reshape(chunks, LANES),
        route_ids,
        route_logit,
        w_gate,
        w_up,
        w_down,
    )
    return layer_out, arrived


def solution(mesh):
    rows = P(("groups", "dev"), None)
    pages = P(("groups", "dev"), None, None)
    placed = (rows, rows, pages, rows, rows, rows, rows, rows, P(), rows, rows)
    placed += (P(None, "dev"), P(None, "dev"), P("dev", None))
    return jax.shard_map(
        on_device, mesh=mesh, in_specs=placed, out_specs=(rows, pages), check_vma=False
    )
```

time: 222 us -> 52.2 us (0.24)
  waiting for transfers between devices: 108 us -> 0 us
  Pallas kernels: 0 us -> 44.5 us
  other arithmetic: 28.6 us -> 0 us
  blocking collectives: 22.2 us -> 0 us
  between operations: 20.9 us -> 0.64 us
  starting transfers between devices: 16.7 us -> 0 us
  local copies, waits for them, and re-layouts: 17.8 us -> 6.81 us
  matrix products: 7.23 us -> 0 us
    unnamed x2 -> x0, waiting for transfers between devices: 87.7 us -> none
    pallas_call x0 -> x1, Pallas kernels: none -> 44.5 us  [on_device(): pl.pallas_call(functools.partial(layer_kernel, n, bits, maxp), out_shape=...]
    all_gather x1 -> x0, blocking collectives: 22.2 us -> none  [on_device(): row_piece = lax.all_gather(normed, 'dev', axis=0, tiled=True)]
    ppermute x18 -> x0, waiting for transfers between devices: 19.9 us -> none  [swapped(): return lax.ppermute(block, axis, route)]
    ppermute x18 -> x0, starting transfers between devices: 16.7 us -> none  [swapped(): return lax.ppermute(block, axis, route)]
    another operation x19 -> x0, other arithmetic: 14.4 us -> none
    scatter x6 -> x0, other arithmetic: 8.91 us -> none  [the longest x3 4.65 us: on_device(): cache_row_block = cache_row_block.at[slot_index].set(received[0])]
    dot_general x5 -> x0, matrix products: 7.23 us -> none  [the longest x1 3.23 us: on_device(): jnp.dot(acts, w_down, preferred_element_type=jnp.float32)]
  transfers between devices with their start and end apart: 19 -> 0, of which waited for: 7 -> 0; matrix products, arithmetic and copies ran while one was open for 19% -> 0% of each run, Pallas kernels for 0% -> 0%
where the time goes in v1:
time: 52.2 us; the launch traced here: 51.9 us
  Pallas kernels  44.5 us (85%)
  local copies, waits for them, and re-layouts  6.81 us (13%)
  between operations  0.64 us (1%)
    pallas_call x1, Pallas kernels, on_device(): pl.pallas_call(functools.partial(layer_kernel, n, bits, maxp), out_shape=...  44.5 us
    unnamed x4, local copies, waits for them, and re-layouts  6.81 us

profile of v1, /device:TPU:0, one launch (start us, length us, event | category | flops | bytes accessed | tf_op | source)
XLA Modules:
  0.0 51.9 jit_solution(14541388387009065986)
XLA Ops:
  0.6 1.3 %copy.17.logit_ref = bf16[3,2]{1,0:T(4,128)(2,1)} copy(bf16[3,2]{0,1:T(2,128)(2,1)} %param.24) | data formatting | bytes 24 | tf_op args[10]
  1.9 1.3 %copy.16.ids_ref = s32[3,2]{1,0:T(4,128)} copy(s32[3,2]{0,1:T(2,128)} %param.23) | data formatting | bytes 48 | tf_op args[9]
  3.3 44.5 %shard_map.149 = (bf16[3,6144]{1,0:T(4,128)(2,1)}, bf16[3,128,2048]{2,1,0:T(8,128)(2,1)}) custom-call(bf16[3,6144]{1,0:T(4,128)(2,1)} %q_ref.1, bf16[3,2048]{1,0:T(4,128)(2,1)} %nkv_ref.1, bf16[14,16,2048]{2,1,0:T(8,128)(2,1)} %pool_hbm.1, s32[1,14]{1,0:T(1,128)} %table.1, s32[1,3]{1,0:T(1,128)} %counts.1, s32[1,3]{1,0:T(1,128)} %fills.1, s32[1,3]{1,0:T(1,128)} %mig.1, ...), custom_call_target="tpu_custom_call" | custom-call | tf_op jit(solution)/shard_map/pallas_call | solution.py:364
  47.8 1.4 %copy.20 = bf16[3,6144]{1,0:T(4,128)(2,1)} copy(bf16[3,6144]{1,0:T(4,128)(2,1)} %get-tuple-element.4) | data formatting | bytes 73728
  49.2 2.7 %copy.21 = bf16[3,128,2048]{2,1,0:T(8,128)(2,1)} copy(bf16[3,128,2048]{2,1,0:T(8,128)(2,1)} %get-tuple-element.5) | data formatting | bytes 3145728

commit v2 on v1

--- a/solution.py
+++ b/solution.py
@@ -11,6 +11,8 @@
 LANES = 128
 NBITS = 3
 REQ = 3
+CACHE_CUTS = ((0, 8), (0, 2, 6, 8), (0, 2, 6, 8))
+CACHE_PARTS = 3
 
 epsilon = 1e-05
 
@@ -47,7 +49,6 @@
     qs,
     kvs,
     rs,
-    route,
     hid_send,
     hid_recv,
     gathered,
@@ -89,7 +90,8 @@
 
     barrier = pltpu.get_barrier_semaphore()
     partners = [flipped(me, 1 << k) for k in range(bits)]
-    for partner in partners:
+    diagonal = flipped(partners[1], 4)
+    for partner in partners + [diagonal]:
         pl.semaphore_signal(
             barrier, inc=1, device_id={"dev": partner}, device_id_type=pl.DeviceIdType.MESH
         )
@@ -107,11 +109,10 @@
     for c in range(kvc):
         kvs[pl.ds(c, REQ, stride=kvc), :] = kf[:, c * LANES : (c + 1) * LANES]
     logits = logit_ref[...].astype(jnp.float32)
-    e = jnp.exp(logits - jnp.max(logits, axis=1, keepdims=True))
-    probs = e / jnp.sum(e, axis=1, keepdims=True)
-    chosen = jnp.sum(jnp.where(ids_ref[...] == 0, probs, 0.0), axis=1, keepdims=True)
-    route[...] = jnp.zeros_like(route)
-    route[pl.ds(0, REQ), :] = jnp.broadcast_to(chosen, (REQ, LANES))
+    e = jnp.exp(logits - jnp.max(logits, axis=0, keepdims=True))
+    probs = e / jnp.sum(e, axis=0, keepdims=True)
+    chosen = jnp.sum(jnp.where(ids_ref[...] == 0, probs, 0.0), axis=0, keepdims=True)
+    route = [jnp.broadcast_to(chosen[:, s : s + 1], (8, LANES)) for s in range(REQ)]
 
     def picked(slot, values):
         chosen_value = values[REQ - 1]
@@ -144,22 +145,30 @@
     choosers = [chooser(b) for b in range(NBITS)]
 
     pool_copy.wait()
-    pl.semaphore_wait(barrier, bits)
+    pl.semaphore_wait(barrier, bits + 1)
 
     cache_copies = {}
     for b in (1, 2, 0):
         cache[b] = jnp.dot(
             choosers[b], pool[...].reshape(pool_rows, width), preferred_element_type=jnp.float32
         ).astype(jnp.bfloat16)
-        cache_copies[b] = pltpu.make_async_remote_copy(
-            src_ref=cache.at[b],
-            dst_ref=arr_ref.at[b],
-            send_sem=cache_send_sem.at[b],
-            recv_sem=cache_recv_sem.at[b],
-            device_id={"dev": partners[b]},
-            device_id_type=pl.DeviceIdType.MESH,
-        )
-        cache_copies[b].start()
+        cuts = CACHE_CUTS[b]
+        for part in range(len(cuts) - 1):
+            rows = pl.ds(cuts[part] * page, (cuts[part + 1] - cuts[part]) * page)
+            cache_copies[b, part] = pltpu.make_async_remote_copy(
+                src_ref=cache.at[b, rows],
+                dst_ref=arr_ref.at[b, rows],
+                send_sem=cache_send_sem.at[b, part],
+                recv_sem=cache_recv_sem.at[b, part],
+                device_id={"dev": partners[b]},
+                device_id_type=pl.DeviceIdType.MESH,
+            )
+        cache_copies[b, 0].start()
+
+    def start_caches(part):
+        for b in (1, 2, 0):
+            if (b, part) in cache_copies:
+                cache_copies[b, part].start()
 
     head = lax.broadcasted_iota(jnp.int32, (chunks, LANES), 0)
     position = lax.broadcasted_iota(jnp.int32, (chunks, maxp * page), 1)
@@ -215,9 +224,7 @@
             jnp.bfloat16
         )
         hid_send[b, pl.ds(0, chunks), :] = hidden
-        hid_send[b, pl.ds(chunks, 8), :] = jnp.broadcast_to(
-            picked(slot, [route[s : s + 1, :] for s in range(REQ)]), (8, LANES)
-        )
+        hid_send[b, pl.ds(chunks, 8), :] = picked(slot, route)
         copy = pltpu.make_async_remote_copy(
             src_ref=hid_send.at[b],
             dst_ref=hid_recv.at[b],
@@ -240,31 +247,68 @@
 
         lax.fori_loop(0, amount, one, 0)
 
-    ag_copies = []
-    for step in range(bits):
-        k = bits - 1 - step
-        size = 1 << step
+    def remote(src, dst, send, recv, index, device):
+        copy = pltpu.make_async_remote_copy(
+            src_ref=src,
+            dst_ref=dst,
+            send_sem=send.at[index],
+            recv_sem=recv.at[index],
+            device_id={"dev": device},
+            device_id_type=pl.DeviceIdType.MESH,
+        )
+        copy.start()
+        return copy
+
+    def at(first, amount):
+        return pl.ds(pl.multiple_of(first * block, 16), amount * block)
+
+    def gather_to(index, first, amount, device):
+        rows = gathered.at[at(first, amount), :]
+        copy = remote(rows, rows, ag_send_sem, ag_recv_sem, index, device)
+        sends.append(copy)
+        return copy
+
+    sends = []
+    quarter = n // 8
+    near, beside = partners[2], partners[1]
+    core = [gather_to(0, pos, 1, partners[0])]
+    core_from = [(flipped(pos, n // 2), 1)]
+    size = 1
+    for step in range(bits - 3):
         have = (pos // size) * size
-        rows = pl.ds(pl.multiple_of(have * block, 16), size * block)
-        copy = pltpu.make_async_remote_copy(
-            src_ref=gathered.at[rows, :],
-            dst_ref=gathered.at[rows, :],
-            send_sem=ag_send_sem.at[step],
-            recv_sem=ag_recv_sem.at[step],
-            device_id={"dev": partners[k]},
-            device_id_type=pl.DeviceIdType.MESH,
-        )
-        copy.start()
-        ag_copies.append(copy)
+        other = flipped(pos // size, 1) * size
+        copy = gather_to(1 + step, have, size, partners[bits - 1 - step])
         if step == 0:
             for hid in hid_copies:
                 hid.start()
             widen(pos, 1)
-        else:
-            widen(other, size // 2)
-        copy.wait_recv()
-        other = flipped(have // size, 1) * size
-    widen(other, n // 2)
+        copy.wait_recv()
+        core.append(gather_to(bits + step, other, size, partners[0]))
+        core_from.append((flipped(other, n // 2), size))
+        widen(other, size)
+        size *= 2
+    have = (pos // quarter) * quarter
+    next_at = flipped(have, quarter)
+    beside_at = flipped(have, 2 * quarter)
+    cross_at = flipped(next_at, 2 * quarter)
+    last = 2 * bits
+    arriving = [
+        (gather_to(last, have, quarter, diagonal), cross_at),
+        (gather_to(last + 1, have, quarter, beside), beside_at),
+        (gather_to(last + 2, have, quarter, near), next_at),
+    ]
+    for (first, amount), copy in zip(core_from, core):
+        copy.wait_recv()
+        widen(first, amount)
+    core = []
+    for i, (copy, where) in enumerate(reversed(arriving)):
+        copy.wait_recv()
+        core.append((gather_to(last + 3 + i, where, quarter, partners[0]), flipped(where, n // 2)))
+        widen(where, quarter)
+    start_caches(1)
+    for copy, where in core:
+        copy.wait_recv()
+        widen(where, quarter)
 
     count = n * REQ
     for c in range(chunks):
@@ -286,30 +330,53 @@
         for j in range(piece):
             shares[pl.ds(c + j, count, stride=chunks), :] = y[:, j * LANES : (j + 1) * LANES]
 
-    rs_copies = []
-    offset = 0
-    for k in range(bits):
+    def cast(first, amount, slot):
+        slab = pl.ds(slot * block, amount * block)
+        rs_send[slab, :] = shares[at(first, amount), :].astype(jnp.bfloat16)
+
+    def scatter_to(index, slot, amount, device):
+        slab = pl.ds(slot * block, amount * block)
+        copy = remote(
+            rs_send.at[slab, :], rs_recv.at[slab, :], rs_send_sem, rs_recv_sem, index, device
+        )
+        sends.append(copy)
+        return copy
+
+    def arrived_rows(slot, amount):
+        return rs_recv[pl.ds(slot * block, amount * block), :].astype(jnp.float32)
+
+    half = n // 2
+    cast(flipped(pos // half, 1) * half, half, 0)
+    copy = scatter_to(0, 0, half, partners[0])
+    copy.wait_recv()
+    base = (pos // half) * half
+    slot = half
+    arriving = []
+    for i, (where, device) in enumerate(
+        ((cross_at, diagonal), (beside_at, beside), (next_at, near))
+    ):
+        from_core = rs_recv[at(where - base, quarter), :].astype(jnp.float32)
+        slab = pl.ds(slot * block, quarter * block)
+        rs_send[slab, :] = (shares[at(where, quarter), :] + from_core).astype(jnp.bfloat16)
+        arriving.append((scatter_to(1 + i, slot, quarter, device), slot))
+        slot += quarter
+    keep = at(have, quarter)
+    shares[keep, :] = shares[keep, :] + rs_recv[at(have - base, quarter), :].astype(jnp.float32)
+    for copy, _ in arriving:
+        copy.wait_recv()
+    start_caches(2)
+    total = shares[keep, :]
+    for _, where in arriving:
+        total = total + arrived_rows(where, quarter)
+    shares[keep, :] = total
+    for k in range(3, bits):
         half = n >> (k + 1)
         mine_at = (pos // half) * half
-        theirs_at = flipped(pos // half, 1) * half
-        slab = pl.ds(offset * block, half * block)
-        rs_send[slab, :] = shares[
-            pl.ds(pl.multiple_of(theirs_at * block, 16), half * block), :
-        ].astype(jnp.bfloat16)
-        copy = pltpu.make_async_remote_copy(
-            src_ref=rs_send.at[slab, :],
-            dst_ref=rs_recv.at[slab, :],
-            send_sem=rs_send_sem.at[k],
-            recv_sem=rs_recv_sem.at[k],
-            device_id={"dev": partners[k]},
-            device_id_type=pl.DeviceIdType.MESH,
-        )
-        copy.start()
-        rs_copies.append(copy)
-        copy.wait_recv()
-        keep = pl.ds(pl.multiple_of(mine_at * block, 16), half * block)
-        shares[keep, :] = shares[keep, :] + rs_recv[slab, :].astype(jnp.float32)
-        offset += half
+        cast(flipped(pos // half, 1) * half, half, slot)
+        copy = scatter_to(1 + k, slot, half, partners[k])
+        copy.wait_recv()
+        shares[at(mine_at, half), :] = shares[at(mine_at, half), :] + arrived_rows(slot, half)
+        slot += half
 
     done = []
     for b in range(NBITS):
@@ -324,10 +391,10 @@
             jnp.bfloat16
         )
 
-    for copy in ag_copies + rs_copies + hid_copies:
+    for copy in sends + hid_copies:
         copy.wait_send()
-    for b in range(NBITS):
-        cache_copies[b].wait()
+    for copy in cache_copies.values():
+        copy.wait()
 
 
 def on_device(
@@ -381,7 +448,6 @@
             pltpu.VMEM((block, LANES), f32),
             pltpu.VMEM((REQ * kvc, LANES), f32),
             pltpu.VMEM((block, LANES), f32),
-            pltpu.VMEM((8, LANES), f32),
             pltpu.VMEM((NBITS, chunks + 8, LANES), f32),
             pltpu.VMEM((NBITS, chunks + 8, LANES), f32),
             pltpu.VMEM((rows, LANES), bf16),
@@ -392,14 +458,14 @@
             pltpu.VMEM(((n - 1) * block, LANES), bf16),
             pltpu.VMEM((block, LANES), f32),
             dma((4,)),
+            dma((NBITS, CACHE_PARTS)),
+            dma((NBITS, CACHE_PARTS)),
             dma((NBITS,)),
             dma((NBITS,)),
-            dma((NBITS,)),
-            dma((NBITS,)),
-            dma((bits,)),
-            dma((bits,)),
-            dma((bits,)),
-            dma((bits,)),
+            dma((2 * bits + 6,)),
+            dma((2 * bits + 6,)),
+            dma((bits + 1,)),
+            dma((bits + 1,)),
         ],
         compiler_params=pltpu.CompilerParams(
             collective_id=0, has_side_effects=True, vmem_limit_bytes=56 * 1024 * 1024
@@ -414,8 +480,8 @@
         mig_slot,
         residual,
         norm_gain.reshape(chunks, LANES),
-        route_ids,
-        route_logit,
+        route_ids.T,
+        route_logit.T,
         w_gate,
         w_up,
         w_down,

time: 52.2 us -> 36.8 us (0.70)
  Pallas kernels: 44.5 us -> 31.7 us
  local copies, waits for them, and re-layouts: 6.81 us -> 4.16 us
    pallas_call x1, Pallas kernels: 44.5 us -> 31.7 us  [on_device(): pl.pallas_call(functools.partial(layer_kernel, n, bits, maxp), out_shape=...]
    unnamed x4 -> x2, local copies, waits for them, and re-layouts: 6.81 us -> 4.16 us
where the time goes in v2:
time: 36.8 us; the launch traced here: 36.5 us
  Pallas kernels  31.7 us (86%)
  local copies, waits for them, and re-layouts  4.16 us (11%)
  between operations  0.64 us (2%)
    pallas_call x1, Pallas kernels, on_device(): pl.pallas_call(functools.partial(layer_kernel, n, bits, maxp), out_shape=...  31.7 us
    unnamed x2, local copies, waits for them, and re-layouts  4.16 us

profile of v2, /device:TPU:0, one launch (start us, length us, event | category | flops | bytes accessed | tf_op | source)
XLA Modules:
  0.0 36.5 jit_solution(6655896975470883038)
XLA Ops:
  0.6 31.7 %shard_map.149 = (bf16[3,6144]{1,0:T(4,128)(2,1)}, bf16[3,128,2048]{2,1,0:T(8,128)(2,1)}) custom-call(bf16[3,6144]{1,0:T(4,128)(2,1)} %q_ref.1, bf16[3,2048]{1,0:T(4,128)(2,1)} %nkv_ref.1, bf16[14,16,2048]{2,1,0:T(8,128)(2,1)} %pool_hbm.1, s32[1,14]{1,0:T(1,128)} %table.1, s32[1,3]{1,0:T(1,128)} %counts.1, s32[1,3]{1,0:T(1,128)} %fills.1, s32[1,3]{1,0:T(1,128)} %mig.1, ...), custom_call_target="tpu_custom_call" | custom-call | tf_op jit(solution)/shard_map/pallas_call | solution.py:431
  32.3 1.4 %copy.18 = bf16[3,6144]{1,0:T(4,128)(2,1)} copy(bf16[3,6144]{1,0:T(4,128)(2,1)} %get-tuple-element.4) | data formatting | bytes 73728
  33.8 2.7 %copy.19 = bf16[3,128,2048]{2,1,0:T(8,128)(2,1)} copy(bf16[3,128,2048]{2,1,0:T(8,128)(2,1)} %get-tuple-element.5) | data formatting | bytes 3145728

commit v3 on v2

--- a/solution.py
+++ b/solution.py
@@ -322,13 +322,18 @@
     up = jnp.dot(x, wu[...], preferred_element_type=jnp.float32)
     acts = (gate * (1.0 / (1.0 + jnp.exp(-gate))) * up).astype(jnp.bfloat16)
     weight_copies[2].wait()
+    wide[pl.ds(0, count), :] = acts.astype(jnp.float32)
     piece = 4
-    for c in range(0, chunks, piece):
-        y = jnp.dot(
-            acts, wd[:, c * LANES : (c + piece) * LANES], preferred_element_type=jnp.float32
-        )
-        for j in range(piece):
-            shares[pl.ds(c + j, count, stride=chunks), :] = y[:, j * LANES : (j + 1) * LANES]
+
+    def share_rows(first, amount):
+        some = wide[pl.ds(pl.multiple_of(first * REQ, 8), amount * REQ), :].astype(jnp.bfloat16)
+        for c in range(0, chunks, piece):
+            y = jnp.dot(
+                some, wd[:, c * LANES : (c + piece) * LANES], preferred_element_type=jnp.float32
+            )
+            for j in range(piece):
+                to = pl.ds(first * block + (c + j), amount * REQ, stride=chunks)
+                shares[to, :] = y[:, j * LANES : (j + 1) * LANES]
 
     def cast(first, amount, slot):
         slab = pl.ds(slot * block, amount * block)
@@ -346,8 +351,10 @@
         return rs_recv[pl.ds(slot * block, amount * block), :].astype(jnp.float32)
 
     half = n // 2
+    share_rows(flipped(pos // half, 1) * half, half)
     cast(flipped(pos // half, 1) * half, half, 0)
     copy = scatter_to(0, 0, half, partners[0])
+    share_rows((pos // half) * half, half)
     copy.wait_recv()
     base = (pos // half) * half
     slot = half
@@ -486,7 +493,27 @@
         w_up,
         w_down,
     )
-    return layer_out, arrived
+    return finish(layer_out, arrived)
+
+
+def finish_kernel(layer_in, arrived_in, layer_out, arrived_out):
+    layer_out[...] = layer_in[...]
+    arrived_out[...] = arrived_in[...]
+
+
+def finish(layer, arrived):
+    flat = pl.BlockSpec(layer.shape, lambda b: (0, 0))
+    one = pl.BlockSpec((1,) + arrived.shape[1:], lambda b: (b, 0, 0))
+    return pl.pallas_call(
+        finish_kernel,
+        grid=(arrived.shape[0],),
+        out_shape=(
+            jax.ShapeDtypeStruct(layer.shape, layer.dtype),
+            jax.ShapeDtypeStruct(arrived.shape, arrived.dtype),
+        ),
+        in_specs=[flat, one],
+        out_specs=(flat, one),
+    )(layer, arrived)
 
 
 def solution(mesh):

time: 36.8 us -> 35.8 us (0.973)
  local copies, waits for them, and re-layouts: 4.16 us -> 0 us
  Pallas kernels: 31.7 us -> 34.9 us
    unnamed x2 -> x0, local copies, waits for them, and re-layouts: 4.16 us -> none
    pallas_call x0 -> x1, Pallas kernels: none -> 3.39 us  [finish(): pl.pallas_call(finish_kernel, grid=(arrived.shape[0],), out_shape=(jax.Sh...]
where the time goes in v3:
time: 35.8 us; the launch traced here: 35.6 us
  Pallas kernels  34.9 us (97%)
  between operations  0.64 us (2%)
    pallas_call x1, Pallas kernels, on_device(): pl.pallas_call(functools.partial(layer_kernel, n, bits, maxp), out_shape=...  31.5 us
    pallas_call x1, Pallas kernels, finish(): pl.pallas_call(finish_kernel, grid=(arrived.shape[0],), out_shape=(jax.Sh...  3.39 us

profile of v3, /device:TPU:0, one launch (start us, length us, event | category | flops | bytes accessed | tf_op | source)
XLA Modules:
  0.0 35.6 jit_solution(5373440723507269998)
XLA Ops:
  0.6 31.5 %shard_map.149 = (bf16[3,6144]{1,0:T(4,128)(2,1)}, bf16[3,128,2048]{2,1,0:T(8,128)(2,1)}) custom-call(bf16[3,6144]{1,0:T(4,128)(2,1)} %q_ref.1, bf16[3,2048]{1,0:T(4,128)(2,1)} %nkv_ref.1, bf16[14,16,2048]{2,1,0:T(8,128)(2,1)} %pool_hbm.1, s32[1,14]{1,0:T(1,128)} %table.1, s32[1,3]{1,0:T(1,128)} %counts.1, s32[1,3]{1,0:T(1,128)} %fills.1, s32[1,3]{1,0:T(1,128)} %mig.1, ...), custom_call_target="tpu_custom_call" | custom-call | tf_op jit(solution)/shard_map/pallas_call | solution.py:438
  32.2 3.4 %shard_map.150 = (bf16[3,6144]{1,0:T(4,128)(2,1)}, bf16[3,128,2048]{2,1,0:T(8,128)(2,1)}) custom-call(bf16[3,6144]{1,0:T(4,128)(2,1)} %get-tuple-element.4.layer_in, bf16[3,128,2048]{2,1,0:T(8,128)(2,1)} %get-tuple-element.5.arrived_in), custom_call_target="tpu_custom_call" | custom-call | tf_op jit(solution)/shard_map/pallas_call | solution.py:507
